TPU v7x, 32 devices: a whole 2x2x4 slice. The times are simulated.
32 devices in a mesh: replica: 2 (over y), tensor: 8 (over z, x), dp: 2 (over core).
Axes of the slice: x: 2, y: 2, z: 4, core: 2. Of those that a mesh axis runs over, the one named last changes fastest.
Arguments:
- queries: bfloat16 [4, 16384], P(('replica', 'dp')), parts along dimension 0, may hold values from -32 to 32
- new_keys: bfloat16 [4, 1024], P(('replica', 'dp')), parts along dimension 0, may hold values from -6 to 6
- new_values: bfloat16 [4, 1024], P(('replica', 'dp')), parts along dimension 0, may hold values from -6 to 6
- key_cache: bfloat16 [4, 256, 1024], P(('replica', 'dp'), 'tensor'), parts along dimension 0, may hold values from -8 to 8
- value_cache: bfloat16 [4, 256, 1024], P(('replica', 'dp'), 'tensor'), parts along dimension 0, may hold values from -6 to 6
- cache_lengths: int32 [4], P(('replica', 'dp')), parts along dimension 0, may hold values from 128 to 256, as said below
- out_weight: bfloat16 [16384, 16384], P('tensor'), may hold values from -0.75 to 0.75
- partial_scales: float32 [4, 128], P(('replica', 'dp')), parts along dimension 0, may hold values from 0.0001 to 0.01
- sum_scales: float32 [4, 128], P(('replica', 'dp')), parts along dimension 0, may hold values from 0.001 to 0.1
Outputs:
- projected: bfloat16 [4, 16384], P(('replica', 'dp')), parts along dimension 0
There are 2 independent parts, one for each index of `replica`. A program takes and returns all parts, laid end to end along the dimension named above; an argument that names none is the same for every part. Nothing has to cross between parts.
Inputs may be any that keep to these rules, and one draw needn't show every extreme that they name: `cache_lengths`: every length is a multiple of 128; in each part one row holds exactly 128 tokens and one exactly 256.
All inputs are finite; a program needn't handle non-finite values.
Results may differ from a plain program's by a relative error of at most 0.02.
Values may be sent and summed in bfloat16 or wider, within the bound.
A program may use at most 192 MiB of HBM per device.

v0:
```python
import math

import jax
import jax.numpy as jnp
from jax import lax
from jax.sharding import PartitionSpec as P

D = 16384
HEADS = 128
KVH = 8
HD = 128
QB = 128


def shards(
    queries,
    new_keys,
    new_values,
    key_cache,
    value_cache,
    cache_lengths,
    out_weight,
    partial_scales,
    sum_scales,
):
    shard_index = lax.axis_index("tensor")
    shard_count = lax.axis_size("tensor")
    row_count = queries.shape[0]
    window = key_cache.shape[1]
    group_size = HEADS // KVH
    heads_here = HEADS // shard_count
    inv_root = 1.0 / math.sqrt(HD)
    query_heads = queries.reshape(row_count, KVH, group_size, HD)
    keys_local = key_cache.reshape(row_count, window, KVH, HD)
    values_local = value_cache.reshape(row_count, window, KVH, HD)
    scores = (
        jnp.einsum("rkgd,rckd->rkgc", query_heads, keys_local, preferred_element_type=jnp.float32)
        * inv_root
    )
    positions = shard_index * window + jnp.arange(window, dtype=jnp.int32)
    live_mask = (positions[None, :] < cache_lengths[:, None])[:, None, None, :]
    masked = jnp.where(live_mask, scores, -1e30)
    local_top = jnp.max(masked, axis=-1)
    weights = jnp.where(live_mask, jnp.exp(masked - local_top[..., None]), 0.0).astype(jnp.bfloat16)
    local_mass = jnp.sum(weights.astype(jnp.float32), axis=-1)
    local_numer = jnp.einsum(
        "rkgc,rckd->rkgd", weights, values_local, preferred_element_type=jnp.float32
    )
    top_parts = local_top.reshape(row_count, HEADS)
    mass_parts = local_mass.reshape(row_count, HEADS)
    numer_parts = local_numer.reshape(row_count, HEADS, HD)
    first_head = shard_index * heads_here
    start_state = (
        jnp.full((row_count, heads_here), -1e30, jnp.float32),
        jnp.zeros((row_count, heads_here), jnp.float32),
        jnp.zeros((row_count, heads_here, HD), jnp.float32),
    )
    piece_top = lax.dynamic_slice_in_dim(
        lax.all_gather(top_parts[None].astype(jnp.bfloat16), "tensor", axis=0, tiled=True).astype(
            jnp.float32
        ),
        first_head,
        heads_here,
        2,
    )
    piece_mass = lax.dynamic_slice_in_dim(
        lax.all_gather(mass_parts[None].astype(jnp.bfloat16), "tensor", axis=0, tiled=True).astype(
            jnp.float32
        ),
        first_head,
        heads_here,
        2,
    )
    piece_numer = lax.dynamic_slice_in_dim(
        lax.all_gather(numer_parts[None].astype(jnp.bfloat16), "tensor", axis=0, tiled=True).astype(
            jnp.float32
        ),
        first_head,
        heads_here,
        2,
    )
    joined_top = jnp.maximum(start_state[0], jnp.max(piece_top, axis=0))
    piece_factor = jnp.exp(piece_top - joined_top)
    carry_factor = jnp.exp(start_state[0] - joined_top)
    joined_mass = start_state[1] * carry_factor + jnp.sum(piece_mass * piece_factor, axis=0)
    joined_numer = start_state[2] * carry_factor[..., None] + jnp.sum(
        piece_numer * piece_factor[..., None], axis=0
    )
    own_query = lax.dynamic_slice_in_dim(queries, first_head * HD, heads_here * HD, 1).reshape(
        row_count, heads_here, HD
    )
    kv_index = (first_head + jnp.arange(heads_here, dtype=jnp.int32)) // group_size
    picker = (kv_index[:, None] == jnp.arange(KVH, dtype=jnp.int32)[None, :]).astype(jnp.float32)
    own_key = jnp.einsum(
        "hk,rkd->rhd",
        picker,
        new_keys.reshape(row_count, KVH, HD).astype(jnp.float32),
        precision=lax.Precision.HIGHEST,
    )
    own_value = jnp.einsum(
        "hk,rkd->rhd",
        picker,
        new_values.reshape(row_count, KVH, HD).astype(jnp.float32),
        precision=lax.Precision.HIGHEST,
    )
    fresh_score = jnp.sum(own_query.astype(jnp.float32) * own_key, axis=-1) * inv_root
    best_score = jnp.maximum(joined_top, fresh_score)
    old_factor = jnp.exp(joined_top - best_score)
    new_factor = jnp.exp(fresh_score - best_score)
    attended = (joined_numer * old_factor[..., None] + new_factor[..., None] * own_value) / (
        joined_mass * old_factor + new_factor
    )[..., None]
    attended = attended.astype(jnp.bfloat16).reshape(row_count, heads_here * HD)
    partial_value = jnp.dot(attended, out_weight, preferred_element_type=jnp.float32)
    block_count = D // QB
    coded_narrow = jnp.clip(
        partial_value.reshape(row_count, block_count, QB) / partial_scales[..., None], -448.0, 448.0
    ).astype(jnp.bfloat16)
    coded_narrow = lax.optimization_barrier(coded_narrow).reshape(row_count, D)
    summed = lax.psum(coded_narrow.astype(jnp.float32), "tensor")
    reduced = summed.reshape(row_count, block_count, QB) * partial_scales[..., None]
    recoded = jnp.clip(reduced / sum_scales[..., None], -448.0, 448.0).astype(jnp.bfloat16)
    gathered = recoded.reshape(row_count, D)
    result = (
        gathered.reshape(row_count, block_count, QB).astype(jnp.float32) * sum_scales[..., None]
    )
    return result.reshape(row_count, D).astype(jnp.bfloat16)


def solution(mesh):
    return jax.shard_map(
        shards,
        mesh=mesh,
        in_specs=(
            P(("replica", "dp"), None),
            P(("replica", "dp"), None),
            P(("replica", "dp"), None),
            P(("replica", "dp"), "tensor", None),
            P(("replica", "dp"), "tensor", None),
            P(("replica", "dp")),
            P("tensor", None),
            P(("replica", "dp"), None),
            P(("replica", "dp"), None),
        ),
        out_specs=P(("replica", "dp"), None),
        check_vma=False,
    )
```

profile of v0, /device:TPU:0, one launch (start us, length us, event | category | flops | bytes accessed | tf_op | source)
XLA Modules:
  0.0 181.5 jit_solution(764068845399228357)
XLA Ops:
  6.5 0.0 copy-start
  6.5 0.0 copy-start.1
  6.5 0.0 copy-start.2
  6.5 0.0 all-reduce.2.cloned.1.call-start
  7.2 0.9 copy.19
  8.1 1.0 reduce.9
  9.1 0.2 fusion.27
  9.4 0.1 convert_element_type.115
  9.5 22.1 %all_gather.9 = bf16[8,1,128]{2,1,0:T(2,128)(2,1)S(1)} all-gather(bf16[1,1,128]{2,1,0:T(2,128)(2,1)S(1)} %convert_element_type.115), channel_id=1, replica_groups=mesh['replica'=2,'tensor'=8,'dp'=2] {'tensor'}, dimensions={0}, use_global_device_ids=true | all-gather | bytes 2304 | tf_op jit(solution)/shard_map/all_gather | solution.py:59
  31.6 0.1 dynamic-slice_reduce_fusion
  31.7 0.2 fusion.19
  31.9 0.1 convert_element_type.123
  32.0 16.2 %all_gather.11 = bf16[8,1,128]{2,1,0:T(2,128)(2,1)S(1)} all-gather(bf16[1,1,128]{2,1,0:T(2,128)(2,1)S(1)} %convert_element_type.123), channel_id=1, replica_groups=mesh['replica'=2,'tensor'=8,'dp'=2] {'tensor'}, dimensions={0}, use_global_device_ids=true | all-gather | bytes 2304 | tf_op jit(solution)/shard_map/all_gather | solution.py:67
  48.1 0.7 dynamic-slice_convert_fusion
  48.8 0.0 copy-done
  48.9 0.9 copy.20
  49.7 0.2 convolution_convert_fusion
  49.9 30.7 %all_gather.10 = bf16[8,1,128,128]{3,2,1,0:T(8,128)(2,1)S(1)} all-gather(bf16[1,1,128,128]{3,2,1,0:T(8,128)(2,1)S(1)} %bitcast.91), channel_id=1, replica_groups=mesh['replica'=2,'tensor'=8,'dp'=2] {'tensor'}, dimensions={0}, use_global_device_ids=true | all-gather | bytes 294912 | tf_op jit(solution)/shard_map/all_gather | solution.py:75
  80.7 0.7 reduce.11
  81.4 0.1 multiply_reduce_fusion.1
  81.5 0.3 fusion.10
  81.8 0.1 multiply_reduce_fusion
  81.9 0.2 fusion.11
  82.1 22.6 %fusion = f32[1,128,128]{2,0,1:T(1,128)S(1)} fusion(bf16[2048,1,1]{0,1,2:T(2,128)(2,1)S(1)} %reshape.335, bf16[2048,16384]{1,0:T(8,128)(2,1)} %param.15), kind=kOutput, calls=%fused_computation | convolution fusion | flops 67108864 | bytes 67178496 | tf_op jit(solution)/shard_map/dot_general | solution.py:114
  104.7 0.0 copy-done.1
  104.7 0.1 fusion.14
  104.8 0.6 convert_element_type.134
  105.5 0.0 all-reduce.2.cloned.1.call-update
  105.5 67.4 %all-reduce.2.cloned.1.call-done = f32[1,16384]{1,0:T(1,128)} async-done(((f32[1,16384]{1,0:T(1,128)}), f32[1,16384]{1,0:T(1,128)}) %all-reduce.2.cloned.1.call-update) | async-done | bytes 65552 | tf_op jit(solution)/shard_map/psum | solution.py:120
  172.9 0.1 div.58
  173.0 0.0 copy-done.2
  173.0 0.1 div.60
  173.1 1.6 multiply_convert_fusion
  (9 shorter events, 0.1 us)
Async XLA Ops:
  6.5 42.3 %copy-start = (bf16[1,1024]{1,0:T(2,128)(2,1)S(1)}, bf16[1,1024]{1,0:T(2,128)(2,1)}, u32[]{:S(2)}) copy-start(bf16[1,1024]{1,0:T(2,128)(2,1)} %param.10) | copy-start | bytes 6148
  6.5 98.2 %copy-start.1 = (f32[1,128]{1,0:T(1,128)S(1)}, f32[1,128]{1,0:T(1,128)}, u32[]{:S(2)}) copy-start(f32[1,128]{1,0:T(1,128)} %param.16) | copy-start | bytes 1540
  6.5 166.4 %copy-start.2 = (f32[1,128]{1,0:T(1,128)S(1)}, f32[1,128]{1,0:T(1,128)}, u32[]{:S(2)}) copy-start(f32[1,128]{1,0:T(1,128)} %param.17) | copy-start | bytes 1540
  6.5 166.4 %all-reduce.2.cloned.1.call-start = ((), (), s32[]{:S(2)}) async-start(), calls=%async_computation | async-start | bytes 131072 | tf_op jit(solution)/shard_map/psum | solution.py:120
Sparse Core Ops, SparseCore 0:
  105.6 67.2 all-reduce.1
where the time goes:
time: 182 us
  blocking collectives  69 us (38%)
  waiting for transfers between devices  67.4 us (37%)
  matrix products  23.5 us (13%)
  between operations  14.2 us (8%)
  other arithmetic  5.28 us (3%)
  local copies, waits for them, and re-layouts  2.05 us (1%)
    psum x1, waiting for transfers between devices, shards(): summed = lax.psum(coded_narrow.astype(jnp.float32), 'tensor')  67.4 us
    all_gather x1, blocking collectives, shards(): lax.all_gather(numer_parts[None].astype(jnp.bfloat16), 'tensor', axis=0,...  30.7 us
    dot_general x1, matrix products, shards(): jnp.dot(attended, out_weight, preferred_element_type=jnp.float32)  22.6 us
    all_gather x1, blocking collectives, shards(): lax.all_gather(top_parts[None].astype(jnp.bfloat16), 'tensor', axis=0, ti...  22.1 us
    all_gather x1, blocking collectives, shards(): lax.all_gather(mass_parts[None].astype(jnp.bfloat16), 'tensor', axis=0, t...  16.2 us
  transfers between devices with their start and end apart: 1, of which 1 were waited for; matrix products, arithmetic and copies ran while one was open for 0% of the time, Pallas kernels for 0%

commit v1 on v0

--- a/solution.py
+++ b/solution.py
@@ -3,6 +3,8 @@
 import jax
 import jax.numpy as jnp
 from jax import lax
+from jax.experimental import pallas as pl
+from jax.experimental.pallas import tpu as pltpu
 from jax.sharding import PartitionSpec as P
 
 D = 16384
@@ -127,9 +129,246 @@
     return result.reshape(row_count, D).astype(jnp.bfloat16)
 
 
+MESH = pl.DeviceIdType.MESH
+QUAD = 4
+GROUP = HEADS // KVH
+CHUNKS = KVH
+CHUNK = D // CHUNKS // QUAD
+BLOCKS = CHUNK // QB
+
+
+def device(row, shard):
+    return {"replica": row // 2, "tensor": shard, "dp": row % 2}
+
+
+def flipped(shard, k):
+    total = 0
+    for bit in (1, 2, 4):
+        a = (shard // bit) % 2
+        b = (k // bit) % 2
+        total = total + bit * (a + b - 2 * a * b)
+    return total
+
+
+def kernel(
+    q_hbm, nk_hbm, nv_hbm, k_hbm, v_hbm, len_hbm, w_hbm, ps_hbm, ss_hbm,
+    out_ref,
+    q_raw, nk, nv, keys, values, lens, first, second, wbuf, q_rows,
+    snd1, rcv1, att, snd2, rcv2, scales, fin, gath,
+    in_sem, w_sem, s1, r1, s2, r2, s3, r3, s4, r4,
+):
+    rep, me, dp = lax.axis_index("replica"), lax.axis_index("tensor"), lax.axis_index("dp")
+    row = rep * 2 + dp
+    window = keys.shape[0]
+    inv_root = 1.0 / math.sqrt(HD)
+
+    small = [
+        pltpu.make_async_copy(a, b, in_sem.at[i])
+        for i, (a, b) in enumerate(
+            [
+                (q_hbm, q_raw), (k_hbm.at[0], keys), (len_hbm, lens), (v_hbm.at[0], values),
+                (nk_hbm, nk), (nv_hbm, nv), (ps_hbm, first), (ss_hbm, second),
+            ]
+        )
+    ]
+    for copy in small:
+        copy.start()
+
+    def weight_copy(i):
+        shard = flipped(me, CHUNKS - 1 - i)
+        start = pl.multiple_of(shard * (QUAD * CHUNK) + row * CHUNK, CHUNK)
+        return pltpu.make_async_copy(w_hbm.at[:, pl.ds(start, CHUNK)], wbuf.at[i], w_sem.at[i])
+
+    for i in range(CHUNKS):
+        weight_copy(i).start()
+
+    barrier = pltpu.get_barrier_semaphore()
+    total_devices = QUAD * CHUNKS
+    place = row * CHUNKS + me
+
+    def greet(j, carry):
+        other = (place + j) % total_devices
+        pl.semaphore_signal(
+            barrier, inc=1, device_id=device(other // CHUNKS, other % CHUNKS), device_id_type=MESH
+        )
+        return carry
+
+    lax.fori_loop(1, total_devices, greet, 0)
+
+    for copy in small:
+        copy.wait()
+
+    for h in range(HEADS):
+        q_rows[h : h + 1, :] = q_raw[0:1, h * HD : (h + 1) * HD].astype(jnp.float32)
+
+    length = lens[0]
+    live = (me * window + lax.broadcasted_iota(jnp.int32, (GROUP, window), 1)) < length
+    lane = lax.broadcasted_iota(jnp.int32, (GROUP, HD), 1)
+    for k in range(KVH):
+        query = q_rows[k * GROUP : (k + 1) * GROUP, :].astype(jnp.bfloat16)
+        score = (
+            lax.dot_general(
+                query, keys[:, k * HD : (k + 1) * HD], (((1,), (1,)), ((), ())),
+                preferred_element_type=jnp.float32,
+            )
+            * inv_root
+        )
+        score = jnp.where(live, score, -1e30)
+        top = jnp.max(score, axis=-1, keepdims=True).astype(jnp.bfloat16).astype(jnp.float32)
+        weight = jnp.where(live, jnp.exp(score - top), 0.0).astype(jnp.bfloat16)
+        mass = jnp.sum(weight.astype(jnp.float32), axis=-1, keepdims=True)
+        numer = jnp.dot(weight, values[:, k * HD : (k + 1) * HD], preferred_element_type=jnp.float32)
+        coarse = mass.astype(jnp.bfloat16).astype(jnp.float32)
+        stats = jnp.where(lane == 0, top, jnp.where(lane == 1, coarse, mass - coarse))
+        snd1[k, 0:GROUP, :] = numer.astype(jnp.bfloat16)
+        snd1[k, GROUP : 2 * GROUP, :] = stats.astype(jnp.bfloat16)
+
+    for i in range(4 * BLOCKS):
+        scales[0, i // BLOCKS, i % BLOCKS, :] = jnp.full((QB,), first[0, me * (QUAD * BLOCKS) + i], jnp.float32)
+        scales[1, i // BLOCKS, i % BLOCKS, :] = jnp.full((QB,), second[0, me * (QUAD * BLOCKS) + i], jnp.float32)
+
+    pl.semaphore_wait(barrier, total_devices - 1)
+
+    for k in range(CHUNKS - 1, 0, -1):
+        shard = flipped(me, k)
+        pltpu.make_async_remote_copy(
+            snd1.at[shard], rcv1.at[me], s1, r1, device_id=device(row, shard), device_id_type=MESH
+        ).start()
+    rcv1[me] = snd1[me]
+    own_query = q_rows[pl.ds(pl.multiple_of(me * GROUP, GROUP), GROUP), :]
+    own = pl.ds(pl.multiple_of(me * HD, HD), HD)
+    own_key = nk[:, own].astype(jnp.float32)
+    own_value = nv[:, own].astype(jnp.float32)
+    fresh = jnp.sum(own_query * own_key, axis=-1, keepdims=True) * inv_root
+    pltpu.make_async_copy(rcv1.at[pl.ds(0, CHUNKS - 1)], rcv1.at[pl.ds(0, CHUNKS - 1)], r1).wait()
+
+    got = [rcv1[t].astype(jnp.float32) for t in range(CHUNKS)]
+    tops = [g[GROUP:, 0:1] for g in got]
+    best = fresh
+    for top in tops:
+        best = jnp.maximum(best, top)
+    fresh_factor = jnp.exp(fresh - best)
+    mass = fresh_factor
+    numer = fresh_factor * own_value
+    for g, top in zip(got, tops):
+        factor = jnp.exp(top - best)
+        mass = mass + factor * (g[GROUP:, 1:2] + g[GROUP:, 2:3])
+        numer = numer + factor * g[:GROUP]
+    mine = pl.ds(pl.multiple_of(row * GROUP, GROUP), GROUP)
+    att[mine, :] = (numer / mass).astype(jnp.bfloat16).astype(jnp.float32)
+
+    for j in range(1, QUAD):
+        pltpu.make_async_remote_copy(
+            att.at[mine], att.at[mine], s2, r2,
+            device_id=device((row + j) % QUAD, me), device_id_type=MESH,
+        ).start()
+    pltpu.make_async_copy(att.at[pl.ds(0, 3 * GROUP)], att.at[pl.ds(0, 3 * GROUP)], r2).wait()
+    x = jnp.concatenate(
+        [att[pl.ds(h, QUAD, stride=GROUP), :] for h in range(GROUP)], axis=1
+    ).astype(jnp.bfloat16)
+
+    def product(i):
+        weight_copy(i).wait()
+        y = jnp.dot(x, wbuf[i], preferred_element_type=jnp.float32)
+        for r in range(QUAD):
+            for b in range(BLOCKS):
+                snd2[i * QUAD + r, b : b + 1, :] = y[r : r + 1, b * QB : (b + 1) * QB]
+
+    def send(i, r, shard):
+        pltpu.make_async_remote_copy(
+            snd2.at[i * QUAD + r], rcv2.at[me * QUAD + row], s3, r3,
+            device_id=device(r, shard), device_id_type=MESH,
+        ).start()
+
+    def step(i, carry):
+        product(i)
+        shard = flipped(me, CHUNKS - 1 - i)
+        for r in range(QUAD):
+            send(i, r, shard)
+        return carry
+
+    lax.fori_loop(0, CHUNKS - 1, step, 0)
+    product(CHUNKS - 1)
+    for j in range(1, QUAD):
+        send(CHUNKS - 1, (row + j) % QUAD, me)
+    rcv2[me * QUAD + row] = snd2[(CHUNKS - 1) * QUAD + row]
+    every = pl.ds(0, total_devices - 1)
+    pltpu.make_async_copy(rcv2.at[every], rcv2.at[every], r3).wait()
+
+    for q in range(QUAD):
+        first_scale, second_scale = scales[0, q], scales[1, q]
+        total = jnp.zeros((BLOCKS, QB), jnp.float32)
+        for t in range(CHUNKS):
+            coded = jnp.clip(rcv2[t * QUAD + q] / first_scale, -448.0, 448.0)
+            total = total + coded.astype(jnp.bfloat16).astype(jnp.float32)
+        recoded = jnp.clip(total * first_scale / second_scale, -448.0, 448.0).astype(jnp.bfloat16)
+        fin[q * BLOCKS : (q + 1) * BLOCKS, :] = recoded.astype(jnp.float32) * second_scale
+    own_rows = pl.ds(pl.multiple_of(me * QUAD * BLOCKS, QUAD * BLOCKS), QUAD * BLOCKS)
+    gath[own_rows, :] = fin[...].astype(jnp.bfloat16)
+
+    for k in range(CHUNKS - 1, 0, -1):
+        pltpu.make_async_remote_copy(
+            gath.at[own_rows], gath.at[own_rows], s4, r4,
+            device_id=device(row, flipped(me, k)), device_id_type=MESH,
+        ).start()
+    pltpu.make_async_copy(snd1.at[pl.ds(0, CHUNKS - 1)], snd1.at[pl.ds(0, CHUNKS - 1)], s1).wait()
+    pltpu.make_async_copy(att.at[pl.ds(0, 3 * GROUP)], att.at[pl.ds(0, 3 * GROUP)], s2).wait()
+    pltpu.make_async_copy(snd2.at[every], snd2.at[every], s3).wait()
+    most = pl.ds(0, (CHUNKS - 1) * QUAD * BLOCKS)
+    pltpu.make_async_copy(gath.at[most], gath.at[most], r4).wait()
+    out_ref[...] = gath[...]
+    pltpu.make_async_copy(gath.at[most], gath.at[most], s4).wait()
+
+
+def fused(*arrays):
+    window = arrays[3].shape[1]
+    depth = arrays[6].shape[0]
+    bf16, f32 = jnp.bfloat16, jnp.float32
+    dma = pltpu.SemaphoreType.DMA
+    out = pl.pallas_call(
+        kernel,
+        out_shape=jax.ShapeDtypeStruct((D // QB, QB), bf16),
+        in_specs=[pl.BlockSpec(memory_space=pl.ANY)] * 9,
+        out_specs=pl.BlockSpec(memory_space=pltpu.VMEM),
+        scratch_shapes=[
+            pltpu.VMEM((1, HEADS * HD), bf16),
+            pltpu.VMEM((1, KVH * HD), bf16),
+            pltpu.VMEM((1, KVH * HD), bf16),
+            pltpu.VMEM((window, KVH * HD), bf16),
+            pltpu.VMEM((window, KVH * HD), bf16),
+            pltpu.SMEM((1,), jnp.int32),
+            pltpu.SMEM((1, D // QB), f32),
+            pltpu.SMEM((1, D // QB), f32),
+            pltpu.VMEM((CHUNKS, depth, CHUNK), bf16),
+            pltpu.VMEM((HEADS, HD), f32),
+            pltpu.VMEM((CHUNKS, 2 * GROUP, HD), bf16),
+            pltpu.VMEM((CHUNKS, 2 * GROUP, HD), bf16),
+            pltpu.VMEM((QUAD * GROUP, HD), f32),
+            pltpu.VMEM((CHUNKS * QUAD, BLOCKS, QB), f32),
+            pltpu.VMEM((CHUNKS * QUAD, BLOCKS, QB), f32),
+            pltpu.VMEM((2, QUAD, BLOCKS, QB), f32),
+            pltpu.VMEM((QUAD * BLOCKS, QB), f32),
+            pltpu.VMEM((D // QB, QB), bf16),
+            dma((8,)), dma((CHUNKS,)),
+            dma, dma, dma, dma, dma, dma, dma, dma,
+        ],
+        compiler_params=pltpu.CompilerParams(
+            collective_id=0, has_side_effects=True, vmem_limit_bytes=48 * 1024 * 1024
+        ),
+    )(*arrays)
+    return out.reshape(1, D)
+
+
+def body_for(mesh):
+    sizes = dict(mesh.shape)
+    if sizes["tensor"] == KVH and sizes["replica"] == 2 and sizes["dp"] == 2:
+        return fused
+    return shards
+
+
 def solution(mesh):
     return jax.shard_map(
-        shards,
+        body_for(mesh),
         mesh=mesh,
         in_specs=(
             P(("replica", "dp"), None),

time: 182 us -> 31.2 us (0.17)
  blocking collectives: 69 us -> 0 us
  waiting for transfers between devices: 67.4 us -> 0 us
  Pallas kernels: 0 us -> 24.3 us
  matrix products: 23.5 us -> 0 us
  between operations: 14.2 us -> 0.67 us
  other arithmetic: 5.28 us -> 0 us
  local copies, waits for them, and re-layouts: 2.05 us -> 5.87 us
    all_gather x3 -> x0, blocking collectives: 69 us -> none  [the longest x1 30.7 us: shards(): lax.all_gather(numer_parts[None].astype(jnp.bfloat16), 'tensor', axis=0,...]
    psum x1 -> x0, waiting for transfers between devices: 67.4 us -> none  [shards(): summed = lax.psum(coded_narrow.astype(jnp.float32), 'tensor')]
    pallas_call x0 -> x1, Pallas kernels: none -> 24.3 us  [fused(): pl.pallas_call(kernel, out_shape=jax.ShapeDtypeStruct((D // QB, QB), bf16...]
    dot_general x5 -> x0, matrix products: 23.5 us -> none  [the longest x1 22.6 us: shards(): jnp.dot(attended, out_weight, preferred_element_type=jnp.float32)]
    unnamed x8 -> x15, local copies, waits for them, and re-layouts: 1.72 us -> 5.87 us
    convert_element_type x7 -> x0, other arithmetic: 3.04 us -> none  [the longest x1 1.6 us: shards(): return result.reshape(row_count, D).astype(jnp.bfloat16)]
  transfers between devices with their start and end apart: 1 -> 0, of which waited for: 1 -> 0; matrix products, arithmetic and copies ran while one was open for 0% -> 0% of each run, Pallas kernels for 0% -> 0%
where the time goes in v1:
time: 31.2 us; the launch traced here: 30.9 us
  Pallas kernels  24.3 us (78%)
  local copies, waits for them, and re-layouts  5.87 us (19%)
  between operations  0.67 us (2%)
    pallas_call x1, Pallas kernels, fused(): pl.pallas_call(kernel, out_shape=jax.ShapeDtypeStruct((D // QB, QB), bf16...  24.3 us
    unnamed x15, local copies, waits for them, and re-layouts  5.87 us

profile of v1, /device:TPU:0, one launch (start us, length us, event | category | flops | bytes accessed | tf_op | source)
XLA Modules:
  0.0 30.9 jit_solution(15126498444899621774)
XLA Ops:
  0.7 0.0 copy-start
  0.7 0.8 %copy-done = bf16[1,16384]{1,0:T(2,128)(2,1)S(1)} copy-done((bf16[1,16384]{1,0:T(2,128)(2,1)S(1)}, bf16[1,16384]{1,0:T(2,128)(2,1)}, u32[]{:S(2)}) %copy-start) | copy-done | bytes 32792
  1.5 0.0 copy-start.1
  1.5 0.8 %copy-done.1 = bf16[1,32,1024]{2,1,0:T(8,128)(2,1)S(1)} copy-done((bf16[1,32,1024]{2,1,0:T(8,128)(2,1)S(1)}, bf16[1,32,1024]{2,1,0:T(8,128)(2,1)}, u32[]{:S(2)}) %copy-start.1) | copy-done | bytes 65560
  2.3 0.0 copy-start.2
  2.3 0.8 %copy-done.2 = bf16[1,32,1024]{2,1,0:T(8,128)(2,1)S(1)} copy-done((bf16[1,32,1024]{2,1,0:T(8,128)(2,1)S(1)}, bf16[1,32,1024]{2,1,0:T(8,128)(2,1)}, u32[]{:S(2)}) %copy-start.2) | copy-done | bytes 65560
  3.2 0.0 copy-start.3
  3.2 0.7 %copy-done.3 = bf16[1,1024]{1,0:T(2,128)(2,1)S(1)} copy-done((bf16[1,1024]{1,0:T(2,128)(2,1)S(1)}, bf16[1,1024]{1,0:T(2,128)(2,1)}, u32[]{:S(2)}) %copy-start.3) | copy-done | bytes 2072
  3.9 0.0 copy-start.4
  3.9 0.7 %copy-done.4 = bf16[1,1024]{1,0:T(2,128)(2,1)S(1)} copy-done((bf16[1,1024]{1,0:T(2,128)(2,1)S(1)}, bf16[1,1024]{1,0:T(2,128)(2,1)}, u32[]{:S(2)}) %copy-start.4) | copy-done | bytes 2072
  4.5 0.0 copy-start.5
  4.5 0.7 %copy-done.5 = f32[1,128]{1,0:T(1,128)S(1)} copy-done((f32[1,128]{1,0:T(1,128)S(1)}, f32[1,128]{1,0:T(1,128)}, u32[]{:S(2)}) %copy-start.5) | copy-done | bytes 536
  5.2 0.0 copy-start.6
  5.2 0.7 %copy-done.6 = f32[1,128]{1,0:T(1,128)S(1)} copy-done((f32[1,128]{1,0:T(1,128)S(1)}, f32[1,128]{1,0:T(1,128)}, u32[]{:S(2)}) %copy-start.6) | copy-done | bytes 536
  5.9 24.3 %shard_map.91 = bf16[128,128]{1,0:T(8,128)(2,1)S(1)} custom-call(bf16[1,16384]{1,0:T(2,128)(2,1)S(1)} %copy-done, bf16[1,1024]{1,0:T(2,128)(2,1)S(1)} %copy-done.3, bf16[1,1024]{1,0:T(2,128)(2,1)S(1)} %copy-done.4, bf16[1,32,1024]{2,1,0:T(8,128)(2,1)S(1)} %copy-done.1, bf16[1,32,1024]{2,1,0:T(8,128)(2,1)S(1)} %copy-done.2, s32[1]{0:T(128)S(6)} %copy.13.len_hbm, ...), custom_call_target="tpu_custom_call" | custom-call | tf_op jit(solution)/shard_map/pallas_call | solution.py:328
  30.2 0.7 %copy.12 = bf16[1,1,128,128]{3,1,2,0:T(2,128)(2,1)} copy(bf16[1,1,128,128]{3,2,1,0:T(8,128)(2,1)S(1)} %bitcast.5) | data formatting | bytes 65536
Async XLA Ops:
  0.7 0.8 %copy-start = (bf16[1,16384]{1,0:T(2,128)(2,1)S(1)}, bf16[1,16384]{1,0:T(2,128)(2,1)}, u32[]{:S(2)}) copy-start(bf16[1,16384]{1,0:T(2,128)(2,1)} %q_hbm.1) | copy-start | bytes 98308
  1.5 0.8 %copy-start.1 = (bf16[1,32,1024]{2,1,0:T(8,128)(2,1)S(1)}, bf16[1,32,1024]{2,1,0:T(8,128)(2,1)}, u32[]{:S(2)}) copy-start(bf16[1,32,1024]{2,1,0:T(8,128)(2,1)} %k_hbm.1) | copy-start | bytes 196612
  2.3 0.8 %copy-start.2 = (bf16[1,32,1024]{2,1,0:T(8,128)(2,1)S(1)}, bf16[1,32,1024]{2,1,0:T(8,128)(2,1)}, u32[]{:S(2)}) copy-start(bf16[1,32,1024]{2,1,0:T(8,128)(2,1)} %v_hbm.1) | copy-start | bytes 196612
  3.2 0.7 %copy-start.3 = (bf16[1,1024]{1,0:T(2,128)(2,1)S(1)}, bf16[1,1024]{1,0:T(2,128)(2,1)}, u32[]{:S(2)}) copy-start(bf16[1,1024]{1,0:T(2,128)(2,1)} %nk_hbm.1) | copy-start | bytes 6148
  3.9 0.7 %copy-start.4 = (bf16[1,1024]{1,0:T(2,128)(2,1)S(1)}, bf16[1,1024]{1,0:T(2,128)(2,1)}, u32[]{:S(2)}) copy-start(bf16[1,1024]{1,0:T(2,128)(2,1)} %nv_hbm.1) | copy-start | bytes 6148
  4.5 0.7 %copy-start.5 = (f32[1,128]{1,0:T(1,128)S(1)}, f32[1,128]{1,0:T(1,128)}, u32[]{:S(2)}) copy-start(f32[1,128]{1,0:T(1,128)} %ps_hbm.1) | copy-start | bytes 1540
  5.2 0.7 %copy-start.6 = (f32[1,128]{1,0:T(1,128)S(1)}, f32[1,128]{1,0:T(1,128)}, u32[]{:S(2)}) copy-start(f32[1,128]{1,0:T(1,128)} %ss_hbm.1) | copy-start | bytes 1540

commit v2 on v1

--- a/solution.py
+++ b/solution.py
@@ -130,21 +130,20 @@
 
 
 MESH = pl.DeviceIdType.MESH
-QUAD = 4
+PAIR = 2
 GROUP = HEADS // KVH
-CHUNKS = KVH
-CHUNK = D // CHUNKS // QUAD
-BLOCKS = CHUNK // QB
-
-
-def device(row, shard):
-    return {"replica": row // 2, "tensor": shard, "dp": row % 2}
-
-
-def flipped(shard, k):
+SHARDS = KVH
+PLANES = 4
+HALF = D // PLANES // PAIR
+PIECES = 2
+PIECE = HALF // PIECES
+BLOCKS = HALF // QB
+
+
+def flipped(index, k):
     total = 0
     for bit in (1, 2, 4):
-        a = (shard // bit) % 2
+        a = (index // bit) % 2
         b = (k // bit) % 2
         total = total + bit * (a + b - 2 * a * b)
     return total
@@ -154,13 +153,16 @@
     q_hbm, nk_hbm, nv_hbm, k_hbm, v_hbm, len_hbm, w_hbm, ps_hbm, ss_hbm,
     out_ref,
     q_raw, nk, nv, keys, values, lens, first, second, wbuf, q_rows,
-    snd1, rcv1, att, snd2, rcv2, scales, fin, gath,
+    snd1, rcv1, att, stage, snd2, rcv2, scales, gath,
     in_sem, w_sem, s1, r1, s2, r2, s3, r3, s4, r4,
 ):
     rep, me, dp = lax.axis_index("replica"), lax.axis_index("tensor"), lax.axis_index("dp")
-    row = rep * 2 + dp
+    plane, side = me // 2, me % 2
     window = keys.shape[0]
     inv_root = 1.0 / math.sqrt(HD)
+
+    def device(shard, core):
+        return {"replica": rep, "tensor": shard, "dp": core}
 
     small = [
         pltpu.make_async_copy(a, b, in_sem.at[i])
@@ -171,30 +173,24 @@
             ]
         )
     ]
+
+    def weight_copy(i, p):
+        target = flipped(plane, PLANES - 1 - i)
+        start = pl.multiple_of(target * (PAIR * HALF) + dp * HALF + p * PIECE, PIECE)
+        slot = i * PIECES + p
+        return pltpu.make_async_copy(w_hbm.at[:, pl.ds(start, PIECE)], wbuf.at[slot], w_sem.at[slot])
+
+    barrier = pltpu.get_barrier_semaphore()
+    for k in range(SHARDS - 1, -1, -1):
+        for c in range(PAIR):
+            if k or c:
+                pl.semaphore_signal(
+                    barrier, inc=1, device_id=device(flipped(me, k), (dp + c) % 2), device_id_type=MESH
+                )
     for copy in small:
         copy.start()
-
-    def weight_copy(i):
-        shard = flipped(me, CHUNKS - 1 - i)
-        start = pl.multiple_of(shard * (QUAD * CHUNK) + row * CHUNK, CHUNK)
-        return pltpu.make_async_copy(w_hbm.at[:, pl.ds(start, CHUNK)], wbuf.at[i], w_sem.at[i])
-
-    for i in range(CHUNKS):
-        weight_copy(i).start()
-
-    barrier = pltpu.get_barrier_semaphore()
-    total_devices = QUAD * CHUNKS
-    place = row * CHUNKS + me
-
-    def greet(j, carry):
-        other = (place + j) % total_devices
-        pl.semaphore_signal(
-            barrier, inc=1, device_id=device(other // CHUNKS, other % CHUNKS), device_id_type=MESH
-        )
-        return carry
-
-    lax.fori_loop(1, total_devices, greet, 0)
-
+    for n in range(0, 4):
+        weight_copy(n // PIECES, n % PIECES).start()
     for copy in small:
         copy.wait()
 
@@ -223,26 +219,29 @@
         snd1[k, 0:GROUP, :] = numer.astype(jnp.bfloat16)
         snd1[k, GROUP : 2 * GROUP, :] = stats.astype(jnp.bfloat16)
 
-    for i in range(4 * BLOCKS):
-        scales[0, i // BLOCKS, i % BLOCKS, :] = jnp.full((QB,), first[0, me * (QUAD * BLOCKS) + i], jnp.float32)
-        scales[1, i // BLOCKS, i % BLOCKS, :] = jnp.full((QB,), second[0, me * (QUAD * BLOCKS) + i], jnp.float32)
-
-    pl.semaphore_wait(barrier, total_devices - 1)
-
-    for k in range(CHUNKS - 1, 0, -1):
-        shard = flipped(me, k)
-        pltpu.make_async_remote_copy(
-            snd1.at[shard], rcv1.at[me], s1, r1, device_id=device(row, shard), device_id_type=MESH
-        ).start()
-    rcv1[me] = snd1[me]
+    for i in range(PAIR * BLOCKS):
+        at = plane * (PAIR * BLOCKS) + i
+        scales[0, i : i + 1, :] = jnp.full((1, QB), first[0, at], jnp.float32)
+        scales[1, i : i + 1, :] = jnp.full((1, QB), second[0, at], jnp.float32)
     own_query = q_rows[pl.ds(pl.multiple_of(me * GROUP, GROUP), GROUP), :]
     own = pl.ds(pl.multiple_of(me * HD, HD), HD)
     own_key = nk[:, own].astype(jnp.float32)
     own_value = nv[:, own].astype(jnp.float32)
     fresh = jnp.sum(own_query * own_key, axis=-1, keepdims=True) * inv_root
-    pltpu.make_async_copy(rcv1.at[pl.ds(0, CHUNKS - 1)], rcv1.at[pl.ds(0, CHUNKS - 1)], r1).wait()
-
-    got = [rcv1[t].astype(jnp.float32) for t in range(CHUNKS)]
+
+    pl.semaphore_wait(barrier, SHARDS * PAIR - 1)
+
+    for k in range(SHARDS - 1, 0, -1):
+        shard = flipped(me, k)
+        pltpu.make_async_remote_copy(
+            snd1.at[shard], rcv1.at[me], s1, r1, device_id=device(shard, dp), device_id_type=MESH
+        ).start()
+    for n in range(4, 8):
+        weight_copy(n // PIECES, n % PIECES).start()
+    rcv1[me] = snd1[me]
+    pltpu.make_async_copy(rcv1.at[pl.ds(0, SHARDS - 1)], rcv1.at[pl.ds(0, SHARDS - 1)], r1).wait()
+
+    got = [rcv1[t].astype(jnp.float32) for t in range(SHARDS)]
     tops = [g[GROUP:, 0:1] for g in got]
     best = fresh
     for top in tops:
@@ -254,67 +253,77 @@
         factor = jnp.exp(top - best)
         mass = mass + factor * (g[GROUP:, 1:2] + g[GROUP:, 2:3])
         numer = numer + factor * g[:GROUP]
-    mine = pl.ds(pl.multiple_of(row * GROUP, GROUP), GROUP)
+    mine = pl.ds(pl.multiple_of(dp * GROUP, GROUP), GROUP)
     att[mine, :] = (numer / mass).astype(jnp.bfloat16).astype(jnp.float32)
 
-    for j in range(1, QUAD):
-        pltpu.make_async_remote_copy(
-            att.at[mine], att.at[mine], s2, r2,
-            device_id=device((row + j) % QUAD, me), device_id_type=MESH,
-        ).start()
-    pltpu.make_async_copy(att.at[pl.ds(0, 3 * GROUP)], att.at[pl.ds(0, 3 * GROUP)], r2).wait()
+    swap = pltpu.make_async_remote_copy(
+        att.at[mine], att.at[mine], s2, r2, device_id=device(me, 1 - dp), device_id_type=MESH
+    )
+    swap.start()
+    swap.wait_recv()
     x = jnp.concatenate(
-        [att[pl.ds(h, QUAD, stride=GROUP), :] for h in range(GROUP)], axis=1
+        [att[pl.ds(h, PAIR, stride=GROUP), :] for h in range(GROUP)], axis=1
     ).astype(jnp.bfloat16)
 
     def product(i):
-        weight_copy(i).wait()
-        y = jnp.dot(x, wbuf[i], preferred_element_type=jnp.float32)
-        for r in range(QUAD):
-            for b in range(BLOCKS):
-                snd2[i * QUAD + r, b : b + 1, :] = y[r : r + 1, b * QB : (b + 1) * QB]
+        for p in range(PIECES):
+            weight_copy(i, p).wait()
+            y = jnp.dot(x, wbuf[i * PIECES + p], preferred_element_type=jnp.float32)
+            for b in range(PIECE // QB):
+                at = p * (PIECE // QB) + b
+                for r in range(PAIR):
+                    stage[r, at : at + 1, :] = y[r : r + 1, b * QB : (b + 1) * QB]
+        for r in range(PAIR):
+            snd2[i * PAIR + r] = stage[r].astype(jnp.bfloat16)
+
+    slot = me * PAIR + dp
 
     def send(i, r, shard):
         pltpu.make_async_remote_copy(
-            snd2.at[i * QUAD + r], rcv2.at[me * QUAD + row], s3, r3,
-            device_id=device(r, shard), device_id_type=MESH,
+            snd2.at[i * PAIR + r], rcv2.at[slot], s3, r3,
+            device_id=device(shard, r), device_id_type=MESH,
         ).start()
 
     def step(i, carry):
         product(i)
-        shard = flipped(me, CHUNKS - 1 - i)
-        for r in range(QUAD):
-            send(i, r, shard)
+        target = flipped(plane, PLANES - 1 - i)
+        for r in range(PAIR):
+            send(i, r, target * 2 + 1 - side)
+            send(i, r, target * 2 + side)
         return carry
 
-    lax.fori_loop(0, CHUNKS - 1, step, 0)
-    product(CHUNKS - 1)
-    for j in range(1, QUAD):
-        send(CHUNKS - 1, (row + j) % QUAD, me)
-    rcv2[me * QUAD + row] = snd2[(CHUNKS - 1) * QUAD + row]
-    every = pl.ds(0, total_devices - 1)
-    pltpu.make_async_copy(rcv2.at[every], rcv2.at[every], r3).wait()
-
-    for q in range(QUAD):
-        first_scale, second_scale = scales[0, q], scales[1, q]
+    lax.fori_loop(0, PLANES - 1, step, 0)
+    last = PLANES - 1
+    product(last)
+    send(last, 0, plane * 2 + 1 - side)
+    send(last, 1, plane * 2 + 1 - side)
+    send(last, 1 - dp, me)
+    rcv2[slot] = snd2[last * PAIR + dp]
+    others = pl.ds(0, SHARDS * PAIR - 1)
+    pltpu.make_async_copy(rcv2.at[others], rcv2.at[others], r3).wait()
+
+    rows = PAIR * BLOCKS
+    for h in range(PAIR):
+        part = slice(h * BLOCKS, (h + 1) * BLOCKS)
+        first_scale, second_scale = scales[0, part, :], scales[1, part, :]
         total = jnp.zeros((BLOCKS, QB), jnp.float32)
-        for t in range(CHUNKS):
-            coded = jnp.clip(rcv2[t * QUAD + q] / first_scale, -448.0, 448.0)
+        for t in range(SHARDS):
+            coded = jnp.clip(rcv2[t * PAIR + h].astype(jnp.float32) / first_scale, -448.0, 448.0)
             total = total + coded.astype(jnp.bfloat16).astype(jnp.float32)
         recoded = jnp.clip(total * first_scale / second_scale, -448.0, 448.0).astype(jnp.bfloat16)
-        fin[q * BLOCKS : (q + 1) * BLOCKS, :] = recoded.astype(jnp.float32) * second_scale
-    own_rows = pl.ds(pl.multiple_of(me * QUAD * BLOCKS, QUAD * BLOCKS), QUAD * BLOCKS)
-    gath[own_rows, :] = fin[...].astype(jnp.bfloat16)
-
-    for k in range(CHUNKS - 1, 0, -1):
+        at = pl.ds(pl.multiple_of(plane * rows + h * BLOCKS, BLOCKS), BLOCKS)
+        gath[at, :] = (recoded.astype(jnp.float32) * second_scale).astype(jnp.bfloat16)
+
+    own_rows = pl.ds(pl.multiple_of(plane * rows, rows), rows)
+    for k in range(PLANES - 1, 0, -1):
         pltpu.make_async_remote_copy(
             gath.at[own_rows], gath.at[own_rows], s4, r4,
-            device_id=device(row, flipped(me, k)), device_id_type=MESH,
+            device_id=device(flipped(plane, k) * 2 + side, dp), device_id_type=MESH,
         ).start()
-    pltpu.make_async_copy(snd1.at[pl.ds(0, CHUNKS - 1)], snd1.at[pl.ds(0, CHUNKS - 1)], s1).wait()
-    pltpu.make_async_copy(att.at[pl.ds(0, 3 * GROUP)], att.at[pl.ds(0, 3 * GROUP)], s2).wait()
-    pltpu.make_async_copy(snd2.at[every], snd2.at[every], s3).wait()
-    most = pl.ds(0, (CHUNKS - 1) * QUAD * BLOCKS)
+    pltpu.make_async_copy(snd1.at[pl.ds(0, SHARDS - 1)], snd1.at[pl.ds(0, SHARDS - 1)], s1).wait()
+    swap.wait_send()
+    pltpu.make_async_copy(rcv2.at[others], rcv2.at[others], s3).wait()
+    most = pl.ds(0, (PLANES - 1) * rows)
     pltpu.make_async_copy(gath.at[most], gath.at[most], r4).wait()
     out_ref[...] = gath[...]
     pltpu.make_async_copy(gath.at[most], gath.at[most], s4).wait()
@@ -339,21 +348,21 @@
             pltpu.SMEM((1,), jnp.int32),
             pltpu.SMEM((1, D // QB), f32),
             pltpu.SMEM((1, D // QB), f32),
-            pltpu.VMEM((CHUNKS, depth, CHUNK), bf16),
+            pltpu.VMEM((PLANES * PIECES, depth, PIECE), bf16),
             pltpu.VMEM((HEADS, HD), f32),
-            pltpu.VMEM((CHUNKS, 2 * GROUP, HD), bf16),
-            pltpu.VMEM((CHUNKS, 2 * GROUP, HD), bf16),
-            pltpu.VMEM((QUAD * GROUP, HD), f32),
-            pltpu.VMEM((CHUNKS * QUAD, BLOCKS, QB), f32),
-            pltpu.VMEM((CHUNKS * QUAD, BLOCKS, QB), f32),
-            pltpu.VMEM((2, QUAD, BLOCKS, QB), f32),
-            pltpu.VMEM((QUAD * BLOCKS, QB), f32),
+            pltpu.VMEM((SHARDS, 2 * GROUP, HD), bf16),
+            pltpu.VMEM((SHARDS, 2 * GROUP, HD), bf16),
+            pltpu.VMEM((PAIR * GROUP, HD), f32),
+            pltpu.VMEM((PAIR, BLOCKS, QB), f32),
+            pltpu.VMEM((PLANES * PAIR, BLOCKS, QB), bf16),
+            pltpu.VMEM((SHARDS * PAIR, BLOCKS, QB), bf16),
+            pltpu.VMEM((2, PAIR * BLOCKS, QB), f32),
             pltpu.VMEM((D // QB, QB), bf16),
-            dma((8,)), dma((CHUNKS,)),
+            dma((8,)), dma((PLANES * PIECES,)),
             dma, dma, dma, dma, dma, dma, dma, dma,
         ],
         compiler_params=pltpu.CompilerParams(
-            collective_id=0, has_side_effects=True, vmem_limit_bytes=48 * 1024 * 1024
+            collective_id=0, has_side_effects=True, vmem_limit_bytes=64 * 1024 * 1024
         ),
     )(*arrays)
     return out.reshape(1, D)

time: 31.2 us -> 25.9 us (0.83)
  local copies, waits for them, and re-layouts: 5.87 us -> 1.44 us
  Pallas kernels: 24.3 us -> 23.6 us
    unnamed x15 -> x1, local copies, waits for them, and re-layouts: 5.87 us -> 1.44 us
    pallas_call x1, Pallas kernels: 24.3 us -> 23.6 us  [fused(): pl.pallas_call(kernel, out_shape=jax.ShapeDtypeStruct((D // QB, QB), bf16...]
where the time goes in v2:
time: 25.9 us; the launch traced here: 25.7 us
  Pallas kernels  23.6 us (91%)
  local copies, waits for them, and re-layouts  1.44 us (6%)
  between operations  0.66 us (3%)
    pallas_call x1, Pallas kernels, fused(): pl.pallas_call(kernel, out_shape=jax.ShapeDtypeStruct((D // QB, QB), bf16...  23.6 us
    unnamed x1, local copies, waits for them, and re-layouts  1.44 us

profile of v2, /device:TPU:0, one launch (start us, length us, event | category | flops | bytes accessed | tf_op | source)
XLA Modules:
  0.0 25.7 jit_solution(3771966912183036445)
XLA Ops:
  0.7 23.6 %shard_map.91 = bf16[128,128]{1,0:T(8,128)(2,1)} custom-call(bf16[1,16384]{1,0:T(2,128)(2,1)} %q_hbm.1, bf16[1,1024]{1,0:T(2,128)(2,1)} %nk_hbm.1, bf16[1,1024]{1,0:T(2,128)(2,1)} %nv_hbm.1, bf16[1,32,1024]{2,1,0:T(8,128)(2,1)} %k_hbm.1, bf16[1,32,1024]{2,1,0:T(8,128)(2,1)} %v_hbm.1, s32[1]{0:T(128)S(6)} %copy.13.len_hbm, bf16[2048,16384]{1,0:T(8,128)(2,1)} %w_hbm.1, ...), custom_call_target="tpu_custom_call" | custom-call | tf_op jit(solution)/shard_map/pallas_call | solution.py:337
  24.3 1.4 %copy.12 = bf16[1,1,128,128]{3,1,2,0:T(2,128)(2,1)} copy(bf16[1,1,128,128]{3,2,1,0:T(8,128)(2,1)} %bitcast.5) | data formatting | bytes 65536

commit v3 on v2

--- a/solution.py
+++ b/solution.py
@@ -189,7 +189,7 @@
                 )
     for copy in small:
         copy.start()
-    for n in range(0, 4):
+    for n in range(0, 3):
         weight_copy(n // PIECES, n % PIECES).start()
     for copy in small:
         copy.wait()
@@ -236,7 +236,7 @@
         pltpu.make_async_remote_copy(
             snd1.at[shard], rcv1.at[me], s1, r1, device_id=device(shard, dp), device_id_type=MESH
         ).start()
-    for n in range(4, 8):
+    for n in range(3, 8):
         weight_copy(n // PIECES, n % PIECES).start()
     rcv1[me] = snd1[me]
     pltpu.make_async_copy(rcv1.at[pl.ds(0, SHARDS - 1)], rcv1.at[pl.ds(0, SHARDS - 1)], r1).wait()

time: 25.9 us -> 25.3 us (0.977)
  Pallas kernels: 23.6 us -> 23 us
    pallas_call x1, Pallas kernels: 23.6 us -> 23 us  [fused(): pl.pallas_call(kernel, out_shape=jax.ShapeDtypeStruct((D // QB, QB), bf16...]
where the time goes in v3:
time: 25.3 us; the launch traced here: 25.1 us
  Pallas kernels  23 us (91%)
  local copies, waits for them, and re-layouts  1.44 us (6%)
  between operations  0.66 us (3%)
    pallas_call x1, Pallas kernels, fused(): pl.pallas_call(kernel, out_shape=jax.ShapeDtypeStruct((D // QB, QB), bf16...  23 us
    unnamed x1, local copies, waits for them, and re-layouts  1.44 us

profile of v3, /device:TPU:0, one launch (start us, length us, event | category | flops | bytes accessed | tf_op | source)
XLA Modules:
  0.0 25.1 jit_solution(1766286052716330584)
XLA Ops:
  0.7 23.0 %shard_map.91 = bf16[128,128]{1,0:T(8,128)(2,1)} custom-call(bf16[1,16384]{1,0:T(2,128)(2,1)} %q_hbm.1, bf16[1,1024]{1,0:T(2,128)(2,1)} %nk_hbm.1, bf16[1,1024]{1,0:T(2,128)(2,1)} %nv_hbm.1, bf16[1,32,1024]{2,1,0:T(8,128)(2,1)} %k_hbm.1, bf16[1,32,1024]{2,1,0:T(8,128)(2,1)} %v_hbm.1, s32[1]{0:T(128)S(6)} %copy.13.len_hbm, bf16[2048,16384]{1,0:T(8,128)(2,1)} %w_hbm.1, ...), custom_call_target="tpu_custom_call" | custom-call | tf_op jit(solution)/shard_map/pallas_call | solution.py:337
  23.7 1.4 %copy.12 = bf16[1,1,128,128]{3,1,2,0:T(2,128)(2,1)} copy(bf16[1,1,128,128]{3,2,1,0:T(8,128)(2,1)} %bitcast.5) | data formatting | bytes 65536
